TPU v7x, 32 devices: a whole 2x2x4 slice. The times are simulated.
32 devices in a mesh: grp: 2 (over y), gx: 4 (over z), gy: 2 (over x), gz: 2 (over core).
Axes of the slice: x: 2, y: 2, z: 4, core: 2. Of those that a mesh axis runs over, the one named last changes fastest.
Arguments:
- ensemble: bfloat16 [128, 32, 32, 256], P(('grp', 'gx'), 'gy', 'gz'), parts along dimension 0, may hold values from -40 to 40
- wind_field: float32 [3, 128, 32, 32], P(None, ('grp', 'gx'), 'gy', 'gz'), parts along dimension 1, may hold values from -0.5 to 0.5
- obs_value: float32 [128, 32, 16], P(('grp', 'gx'), 'gy', 'gz'), parts along dimension 0, may hold values from -60 to 60
- obs_weight: float32 [128, 32, 16], P(('grp', 'gx'), 'gy', 'gz'), parts along dimension 0, may hold values from 0.1 to 1.75
- obs_cell: int32 [128, 32, 16], P(('grp', 'gx'), 'gy', 'gz'), parts along dimension 0, may hold values from 0 to 4095, as said below
- obs_used: int32 [128, 32, 16], P(('grp', 'gx'), 'gy', 'gz'), parts along dimension 0, may hold values 0 or 1
Outputs:
- analysis: bfloat16 [128, 32, 32, 256], P(('grp', 'gx'), 'gy', 'gz'), parts along dimension 0
There are 2 independent parts, one for each index of `grp`. A program takes and returns all parts, laid end to end along the dimension named above; each array names one. Nothing has to cross between parts.
Inputs may be any that keep to these rules, and one draw needn't show every extreme that they name: `obs_cell`: each entry names a cell of the grid block held by the same device, numbered (x * 16 + y) * 16 + z inside the block.
All inputs are finite; a program needn't handle non-finite values. No bound on the sum of `obs_used` on one device may be relied on, other than what follows from the above.
Results may differ from a plain program's by a relative error of at most 0.0067.
Values may be sent and summed in bfloat16 or wider, within the bound.
A program may use at most 64 MiB of HBM per device.

v0:
```python
import math
import jax
import jax.numpy as jnp
from jax import lax
from jax.sharding import PartitionSpec as P

ITERS = 5
diffusion = 0.1
steepen = 0.1


def padded_2(block, sides, width):
    for axis, dim in sides:
        count = lax.axis_size(axis)
        forward = [(i, i + 1) for i in range(count - 1)]
        backward = [(target, source) for source, target in forward]
        low = lax.ppermute(
            lax.slice_in_dim(block, block.shape[dim] - width, None, axis=dim), axis, forward
        )
        high = lax.ppermute(lax.slice_in_dim(block, 0, width, axis=dim), axis, backward)
        block = jnp.concatenate([low, block, high], axis=dim)
    return block


def advance(padded, wind_field):
    centre = padded[1:-1, 1:-1, 1:-1].astype(jnp.float32)
    ahead_x = padded[2:, 1:-1, 1:-1].astype(jnp.float32)
    behind_x = padded[:-2, 1:-1, 1:-1].astype(jnp.float32)
    ahead_y = padded[1:-1, 2:, 1:-1].astype(jnp.float32)
    behind_y = padded[1:-1, :-2, 1:-1].astype(jnp.float32)
    ahead_z = padded[1:-1, 1:-1, 2:].astype(jnp.float32)
    behind_z = padded[1:-1, 1:-1, :-2].astype(jnp.float32)
    laplace = ahead_x + behind_x + ahead_y + behind_y + ahead_z + behind_z - 6.0 * centre
    transport = (wind_field[0][..., None] + steepen * centre) * (ahead_x - behind_x)
    transport = transport + wind_field[1][..., None] * (ahead_y - behind_y)
    transport = transport + wind_field[2][..., None] * (ahead_z - behind_z)
    return lax.optimization_barrier(
        (centre + diffusion * laplace - 0.5 * transport).astype(jnp.bfloat16)
    )


def product(left, right):
    return jnp.dot(left, right, precision=lax.Precision.HIGHEST)


def inverse_root(gram_full):
    member_states = gram_full.shape[0]
    identity = jnp.eye(member_states, dtype=jnp.float32)
    coupled = identity + gram_full
    frob_norm = jnp.sqrt(jnp.sum(coupled * coupled))
    iterate_y = coupled / frob_norm
    iterate_z = identity
    for sweep in range(ITERS):
        factor_p = 0.5 * (3.0 * identity - product(iterate_z, iterate_y))
        iterate_y = product(factor_p, iterate_y)
        iterate_z = product(factor_p, iterate_z)
    return iterate_z / jnp.sqrt(frob_norm)


def per_device(ensemble, wind_field, obs_value, obs_weight, obs_cell, obs_used):
    extent_x, extent_y, extent_z, member_states = ensemble.shape

    def advance_border(field):
        padded = padded_2(field, (("gx", 0), ("gy", 1), ("gz", 2)), 1)
        return advance(padded, wind_field)

    predicted_state = advance_border(advance_border(ensemble))
    ensemble_average = jnp.mean(predicted_state.astype(jnp.float32), axis=3)
    member_departures = (predicted_state.astype(jnp.float32) - ensemble_average[..., None]).astype(
        jnp.bfloat16
    )
    flat_anom = member_departures.reshape(-1, member_states)
    mean_flat = ensemble_average.reshape(-1)
    obs_spots = obs_cell.reshape(-1)
    picked = jnp.take(flat_anom, obs_spots, axis=0)
    mean_at = jnp.take(mean_flat, obs_spots, axis=0)
    obs_total = obs_cell.size * lax.axis_size("gx") * lax.axis_size("gy") * lax.axis_size("gz")
    in_use = obs_used.reshape(-1).astype(jnp.float32)
    obs_scale = obs_weight.reshape(-1)
    values = obs_value.reshape(-1)
    scaled = (
        (in_use * obs_scale / math.sqrt(obs_total))[:, None] * picked.astype(jnp.float32)
    ).astype(jnp.bfloat16)
    innovation = (in_use * obs_scale * (values - mean_at) / math.sqrt(obs_total)).astype(
        jnp.bfloat16
    )
    gram_part = lax.dot_general(
        scaled, scaled, (((0,), (0,)), ((), ())), preferred_element_type=jnp.float32
    )
    couple_part = jnp.dot(innovation, scaled, preferred_element_type=jnp.float32)
    gram_full, coupling = lax.psum((gram_part, couple_part), ("gx", "gy", "gz"))
    transform = inverse_root(gram_full)
    shift = product(transform, product(transform, coupling))
    weights = (transform + shift[:, None]).astype(jnp.bfloat16)
    mixed = jnp.dot(flat_anom, weights, preferred_element_type=jnp.float32)
    analysis = (mean_flat[:, None] + mixed).astype(jnp.bfloat16)
    return analysis.reshape(extent_x, extent_y, extent_z, member_states)


def solution(mesh):
    in_specs = (
        P(("grp", "gx"), "gy", "gz", None),
        P(None, ("grp", "gx"), "gy", "gz"),
        P(("grp", "gx"), "gy", "gz"),
        P(("grp", "gx"), "gy", "gz"),
        P(("grp", "gx"), "gy", "gz"),
        P(("grp", "gx"), "gy", "gz"),
    )
    out_specs = P(("grp", "gx"), "gy", "gz", None)
    return jax.shard_map(
        per_device, mesh=mesh, in_specs=in_specs, out_specs=out_specs, check_vma=False
    )
```

profile of v0, /device:TPU:1, one launch (start us, length us, event | category | flops | bytes accessed | tf_op | source)
XLA Modules:
  0.0 221.4 jit_solution(8572135581183431103)
XLA Ops:
  6.5 1.0 fusion.37
  7.5 4.0 %collective-permute-start.1 = (bf16[1,16,16,256]{3,2,1,0:T(8,128)(2,1)S(1)}, bf16[1,16,16,256]{3,2,1,0:T(8,128)(2,1)S(1)}, u32[]{:S(2)}, u32[]{:S(2)}) collective-permute-start(bf16[1,16,16,256]{3,2,1,0:T(8,128)(2,1)S(1)} %get-tuple-element.18), channel_id=1, source_target_pairs={{0,4},{4,8},{8,12},{1,5},{5,9},{9,13},{2,6},{6,10},{10,14},{3,7},{... | collective-permute-start | bytes 393224 | tf_op jit(solution)/shard_map/ppermute | solution.py:17
  11.6 1.3 collective-permute-start
  12.9 0.8 collective-permute-done.1
  13.7 1.8 constant_dynamic-update-slice_fusion.1
  15.6 1.7 collective-permute-done
  17.3 1.3 collective-permute-start.2
  18.6 4.0 %collective-permute-start.3 = (bf16[18,1,16,256]{3,2,1,0:T(8,128)(2,1)S(1)}, bf16[18,1,16,256]{3,2,1,0:T(8,128)(2,1)S(1)}, u32[]{:S(2)}, u32[]{:S(2)}) collective-permute-start(bf16[18,1,16,256]{3,2,1,0:T(8,128)(2,1)S(1)} %get-tuple-element.13), channel_id=1, source_target_pairs={{0,2},{1,3},{4,6},{5,7},{8,10},{9,11},{12,14},{13,15},{16,18},{17,... | collective-permute-start | bytes 442376 | tf_op jit(solution)/shard_map/ppermute | solution.py:17
  22.7 0.1 reshape.81
  22.9 0.3 collective-permute-done.2
  23.2 1.5 collective-permute-done.3
  24.7 0.5 pad_maximum_fusion.35
  25.3 5.2 %collective-permute-start.4 = (bf16[18,18,1,256]{3,1,2,0:T(8,128)(2,1)S(1)}, bf16[18,18,1,256]{3,1,2,0:T(8,128)(2,1)S(1)}, u32[]{:S(2)}, u32[]{:S(2)}) collective-permute-start(bf16[18,18,1,256]{3,1,2,0:T(8,128)(2,1)S(1)} %copy.40), channel_id=1, source_target_pairs={{1,0},{3,2},{5,4},{7,6},{9,8},{11,10},{13,12},{15,14},{17,16},{19,... | collective-permute-start | bytes 497672 | tf_op jit(solution)/shard_map/ppermute | solution.py:20
  30.5 1.4 collective-permute-start.5
  32.0 1.1 slice_bitcast_fusion.2
  33.0 0.3 copy.41
  33.3 0.7 collective-permute-done.5
  34.0 0.3 copy.43
  34.3 10.0 %fusion.6 = bf16[16,16,16,256]{3,2,1,0:T(8,128)(2,1)S(1)} fusion(bf16[16,16,16,256]{3,2,1,0:T(8,128)(2,1)S(1)} %copy-done.3, bf16[18,18,1,256]{3,2,1,0:T(2,128)(2,1)S(1)} %copy.43, bf16[18,1,16,256]{3,2,1,0:T(8,128)(2,1)S(1)} %collective-permute-done.2, bf16[18,16,16,256]{3,2,1,0:T(8,128)(2,1)S(1)} %copy-done.2, ...), kind=kLoop, calls=%fused_computation.33 | loop fusion | flops 57671680 | bytes 7491584 | tf_op jit(solution)/shard_map/convert_element_type | solution.py:38
  44.3 1.3 collective-permute-start.6
  45.6 4.0 %collective-permute-start.7 = (bf16[1,16,16,256]{3,2,1,0:T(8,128)(2,1)S(1)}, bf16[1,16,16,256]{3,2,1,0:T(8,128)(2,1)S(1)}, u32[]{:S(2)}, u32[]{:S(2)}) collective-permute-start(bf16[1,16,16,256]{3,2,1,0:T(8,128)(2,1)S(1)} %get-tuple-element.15), channel_id=1, source_target_pairs={{0,4},{4,8},{8,12},{1,5},{5,9},{9,13},{2,6},{6,10},{10,14},{3,7},{... | collective-permute-start | bytes 393224 | tf_op jit(solution)/shard_map/ppermute | solution.py:17
  49.7 1.1 collective-permute-done.6
  50.9 0.9 collective-permute-done.7
  51.8 1.3 collective-permute-start.8
  53.1 4.1 %collective-permute-start.9 = (bf16[18,1,16,256]{3,2,1,0:T(8,128)(2,1)S(1)}, bf16[18,1,16,256]{3,2,1,0:T(8,128)(2,1)S(1)}, u32[]{:S(2)}, u32[]{:S(2)}) collective-permute-start(bf16[18,1,16,256]{3,2,1,0:T(8,128)(2,1)S(1)} %get-tuple-element.11), channel_id=1, source_target_pairs={{0,2},{1,3},{4,6},{5,7},{8,10},{9,11},{12,14},{13,15},{16,18},{17,... | collective-permute-start | bytes 442376 | tf_op jit(solution)/shard_map/ppermute | solution.py:17
  57.2 0.9 convert_multiply_fusion.4
  58.2 0.1 mul.137
  58.3 0.9 copy.54
  59.2 0.1 reshape.82
  59.3 0.7 pad_maximum_fusion.32
  60.1 4.4 %collective-permute-start.10 = (bf16[18,18,1,256]{3,1,2,0:T(8,128)(2,1)S(1)}, bf16[18,18,1,256]{3,1,2,0:T(8,128)(2,1)S(1)}, u32[]{:S(2)}, u32[]{:S(2)}) collective-permute-start(bf16[18,18,1,256]{3,1,2,0:T(8,128)(2,1)S(1)} %copy.44), channel_id=1, source_target_pairs={{1,0},{3,2},{5,4},{7,6},{9,8},{11,10},{13,12},{15,14},{17,16},{19,... | collective-permute-start | bytes 497672 | tf_op jit(solution)/shard_map/ppermute | solution.py:20
  64.6 1.3 collective-permute-start.11
  65.9 0.3 copy.45
  66.2 1.8 collective-permute-done.11
  67.9 0.3 copy.47
  68.2 13.7 %fusion.16 = bf16[16,16,16,256]{3,2,1,0:T(8,128)(2,1)S(1)} fusion(bf16[16,16,16,256]{3,2,1,0:T(8,128)(2,1)S(1)} %fusion.6, bf16[18,18,1,256]{3,2,1,0:T(2,128)(2,1)S(1)} %copy.47, bf16[18,1,16,256]{3,2,1,0:T(8,128)(2,1)S(1)} %collective-permute-done.8, bf16[18,1,16,256]{3,2,1,0:T(8,128)(2,1)S(1)} %collective-permute-done.9, ...), kind=kLoop, calls=%fused_computation.43 | loop fusion | flops 74448896 | bytes 5132288 | tf_op jit(solution)/shard_map/convert_element_type | solution.py:38
  81.9 1.3 copy-done
  83.2 0.6 convert_reduce_fusion
  84.0 1.9 fusion.21
  86.1 9.1 %gather_fusion = bf16[2048,256]{1,0:T(8,128)(2,1)} fusion(bf16[4096,256]{1,0:T(8,128)(2,1)S(1)} %bitcast.48, s32[2048]{0:T(1024)S(1)} %broadcast_clamp_fusion), kind=kCustom, calls=%fused_computation | custom fusion | bytes 2105344 | tf_op jit(solution)/shard_map/jit(_take)/gather | solution.py:75
  95.2 11.8 %gather_fusion.1 = f32[2048]{0:T(1024)S(1)} fusion(f32[4096]{0:T(1024)S(1)} %div.28, s32[2048]{0:T(1024)S(1)} %broadcast_clamp_fusion), kind=kCustom, calls=%fused_computation.1 | custom fusion | bytes 24576 | tf_op jit(solution)/shard_map/jit(_take)/gather | solution.py:76
  107.0 1.8 multiply_convert_fusion
  108.7 1.2 fusion.38
  109.9 0.2 fusion.45
  110.2 31.3 %psum.15 = f32[256]{0:T(256)S(1)} all-reduce(f32[256]{0:T(256)S(1)} %bitcast.53), channel_id=1, replica_groups=mesh['grp'=2,'gx'=4,'gy'=2,'gz'=2] {'gx','gy','gz'}, use_global_device_ids=true, to_apply=%region_3.4 | all-reduce | flops 256 | bytes 2048 | tf_op jit(solution)/shard_map/psum | solution.py:91
  141.5 60.8 %all-reduce.2.cloned.1.call-done = f32[256,256]{1,0:T(8,128)} async-done(((f32[256,256]{1,0:T(8,128)}), f32[256,256]{1,0:T(8,128)}) %all-reduce.2.cloned.1.call-update) | async-done | bytes 262160 | tf_op jit(solution)/shard_map/psum | solution.py:91
  202.3 1.6 multiply_reduce_fusion
  204.6 1.3 fusion.28
  205.9 0.3 fusion.29
  206.2 1.4 fusion.32
  207.5 0.4 fusion.27
  207.9 0.4 fusion.40
  208.3 0.4 fusion.39
  208.7 0.4 fusion.26
  209.1 0.4 fusion.42
  209.5 0.4 fusion.41
  209.9 0.4 fusion.25
  210.3 0.4 fusion.44
  210.6 0.4 fusion.43
  211.1 0.4 fusion.24
  211.5 0.4 convolution_divide_fusion
  211.8 0.3 convolution_bitcast_fusion
  212.1 0.3 fusion.46
  212.4 2.1 fusion
  (35 shorter events, 0.9 us)
Async XLA Ops:
  6.5 195.7 %all-reduce.2.cloned.1.call-start = ((), (), s32[]{:S(2)}) async-start(), calls=%async_computation | async-start | bytes 524288 | tf_op jit(solution)/shard_map/psum | solution.py:91
  7.5 6.2 %collective-permute-start.1 = (bf16[1,16,16,256]{3,2,1,0:T(8,128)(2,1)S(1)}, bf16[1,16,16,256]{3,2,1,0:T(8,128)(2,1)S(1)}, u32[]{:S(2)}, u32[]{:S(2)}) collective-permute-start(bf16[1,16,16,256]{3,2,1,0:T(8,128)(2,1)S(1)} %get-tuple-element.18), channel_id=1, source_target_pairs={{0,4},{4,8},{8,12},{1,5},{5,9},{9,13},{2,6},{6,10},{10,14},{3,7},{... | collective-permute-start | bytes 393224 | tf_op jit(solution)/shard_map/ppermute | solution.py:17
  11.6 5.7 %collective-permute-start = (bf16[1,16,16,256]{3,2,1,0:T(8,128)(2,1)S(1)}, bf16[1,16,16,256]{3,2,1,0:T(8,128)(2,1)S(1)}, u32[]{:S(2)}, u32[]{:S(2)}) collective-permute-start(bf16[1,16,16,256]{3,2,1,0:T(8,128)(2,1)S(1)} %get-tuple-element.17), channel_id=1, source_target_pairs={{4,0},{8,4},{12,8},{5,1},{9,5},{13,9},{6,2},{10,6},{14,10},{7,3},{... | collective-permute-start | bytes 393224 | tf_op jit(solution)/shard_map/ppermute | solution.py:20
  13.7 8.9 %copy-start.4 = (s32[16,16,8]{1,2,0:T(8,128)S(1)}, s32[16,16,8]{1,2,0:T(8,128)}, u32[]{:S(2)}) copy-start(s32[16,16,8]{1,2,0:T(8,128)} %param.10) | copy-start | bytes 24580
  17.3 8.0 %copy-start.1 = (bf16[18,16,16,256]{3,2,1,0:T(8,128)(2,1)}, bf16[18,16,16,256]{3,2,1,0:T(8,128)(2,1)S(1)}, u32[]{:S(2)}) copy-start(bf16[18,16,16,256]{3,2,1,0:T(8,128)(2,1)S(1)} %constant_dynamic-update-slice_fusion) | copy-start | bytes 7077892
  17.3 5.9 %collective-permute-start.2 = (bf16[18,1,16,256]{3,2,1,0:T(8,128)(2,1)S(1)}, bf16[18,1,16,256]{3,2,1,0:T(8,128)(2,1)S(1)}, u32[]{:S(2)}, u32[]{:S(2)}) collective-permute-start(bf16[18,1,16,256]{3,2,1,0:T(8,128)(2,1)S(1)} %get-tuple-element.14), channel_id=1, source_target_pairs={{2,0},{3,1},{6,4},{7,5},{10,8},{11,9},{14,12},{15,13},{18,16},{19,... | collective-permute-start | bytes 442376 | tf_op jit(solution)/shard_map/ppermute | solution.py:20
  18.6 6.1 %collective-permute-start.3 = (bf16[18,1,16,256]{3,2,1,0:T(8,128)(2,1)S(1)}, bf16[18,1,16,256]{3,2,1,0:T(8,128)(2,1)S(1)}, u32[]{:S(2)}, u32[]{:S(2)}) collective-permute-start(bf16[18,1,16,256]{3,2,1,0:T(8,128)(2,1)S(1)} %get-tuple-element.13), channel_id=1, source_target_pairs={{0,2},{1,3},{4,6},{5,7},{8,10},{9,11},{12,14},{13,15},{16,18},{17,... | collective-permute-start | bytes 442376 | tf_op jit(solution)/shard_map/ppermute | solution.py:17
  22.9 11.4 %copy-start.3 = (bf16[16,16,16,256]{3,2,1,0:T(8,128)(2,1)S(1)}, bf16[16,16,16,256]{3,2,1,0:T(8,128)(2,1)}, u32[]{:S(2)}) copy-start(bf16[16,16,16,256]{3,2,1,0:T(8,128)(2,1)} %param.6) | copy-start | bytes 6291460
  25.3 7.7 %collective-permute-start.4 = (bf16[18,18,1,256]{3,1,2,0:T(8,128)(2,1)S(1)}, bf16[18,18,1,256]{3,1,2,0:T(8,128)(2,1)S(1)}, u32[]{:S(2)}, u32[]{:S(2)}) collective-permute-start(bf16[18,18,1,256]{3,1,2,0:T(8,128)(2,1)S(1)} %copy.40), channel_id=1, source_target_pairs={{1,0},{3,2},{5,4},{7,6},{9,8},{11,10},{13,12},{15,14},{17,16},{19,... | collective-permute-start | bytes 497672 | tf_op jit(solution)/shard_map/ppermute | solution.py:20
  30.5 3.8 %copy-start.2 = (bf16[18,16,16,256]{3,2,1,0:T(8,128)(2,1)S(1)}, bf16[18,16,16,256]{3,2,1,0:T(8,128)(2,1)}, u32[]{:S(2)}) copy-start(bf16[18,16,16,256]{3,2,1,0:T(8,128)(2,1)} %copy-done.1) | copy-start | bytes 7077892
  30.5 3.5 %collective-permute-start.5 = (bf16[18,18,1,256]{3,1,2,0:T(8,128)(2,1)S(1)}, bf16[18,18,1,256]{3,1,2,0:T(8,128)(2,1)S(1)}, u32[]{:S(2)}, u32[]{:S(2)}) collective-permute-start(bf16[18,18,1,256]{3,1,2,0:T(8,128)(2,1)S(1)} %copy.42), channel_id=1, source_target_pairs={{0,1},{2,3},{4,5},{6,7},{8,9},{10,11},{12,13},{14,15},{16,17},{18,... | collective-permute-start | bytes 497672 | tf_op jit(solution)/shard_map/ppermute | solution.py:17
  44.3 6.5 %collective-permute-start.6 = (bf16[1,16,16,256]{3,2,1,0:T(8,128)(2,1)S(1)}, bf16[1,16,16,256]{3,2,1,0:T(8,128)(2,1)S(1)}, u32[]{:S(2)}, u32[]{:S(2)}) collective-permute-start(bf16[1,16,16,256]{3,2,1,0:T(8,128)(2,1)S(1)} %get-tuple-element.16), channel_id=1, source_target_pairs={{4,0},{8,4},{12,8},{5,1},{9,5},{13,9},{6,2},{10,6},{14,10},{7,3},{... | collective-permute-start | bytes 393224 | tf_op jit(solution)/shard_map/ppermute | solution.py:20
  45.6 6.1 %collective-permute-start.7 = (bf16[1,16,16,256]{3,2,1,0:T(8,128)(2,1)S(1)}, bf16[1,16,16,256]{3,2,1,0:T(8,128)(2,1)S(1)}, u32[]{:S(2)}, u32[]{:S(2)}) collective-permute-start(bf16[1,16,16,256]{3,2,1,0:T(8,128)(2,1)S(1)} %get-tuple-element.15), channel_id=1, source_target_pairs={{0,4},{4,8},{8,12},{1,5},{5,9},{9,13},{2,6},{6,10},{10,14},{3,7},{... | collective-permute-start | bytes 393224 | tf_op jit(solution)/shard_map/ppermute | solution.py:17
  51.8 7.6 %collective-permute-start.8 = (bf16[18,1,16,256]{3,2,1,0:T(8,128)(2,1)S(1)}, bf16[18,1,16,256]{3,2,1,0:T(8,128)(2,1)S(1)}, u32[]{:S(2)}, u32[]{:S(2)}) collective-permute-start(bf16[18,1,16,256]{3,2,1,0:T(8,128)(2,1)S(1)} %get-tuple-element.12), channel_id=1, source_target_pairs={{2,0},{3,1},{6,4},{7,5},{10,8},{11,9},{14,12},{15,13},{18,16},{19,... | collective-permute-start | bytes 442376 | tf_op jit(solution)/shard_map/ppermute | solution.py:20
  53.1 6.3 %collective-permute-start.9 = (bf16[18,1,16,256]{3,2,1,0:T(8,128)(2,1)S(1)}, bf16[18,1,16,256]{3,2,1,0:T(8,128)(2,1)S(1)}, u32[]{:S(2)}, u32[]{:S(2)}) collective-permute-start(bf16[18,1,16,256]{3,2,1,0:T(8,128)(2,1)S(1)} %get-tuple-element.11), channel_id=1, source_target_pairs={{0,2},{1,3},{4,6},{5,7},{8,10},{9,11},{12,14},{13,15},{16,18},{17,... | collective-permute-start | bytes 442376 | tf_op jit(solution)/shard_map/ppermute | solution.py:17
  60.1 5.8 %collective-permute-start.10 = (bf16[18,18,1,256]{3,1,2,0:T(8,128)(2,1)S(1)}, bf16[18,18,1,256]{3,1,2,0:T(8,128)(2,1)S(1)}, u32[]{:S(2)}, u32[]{:S(2)}) collective-permute-start(bf16[18,18,1,256]{3,1,2,0:T(8,128)(2,1)S(1)} %copy.44), channel_id=1, source_target_pairs={{1,0},{3,2},{5,4},{7,6},{9,8},{11,10},{13,12},{15,14},{17,16},{19,... | collective-permute-start | bytes 497672 | tf_op jit(solution)/shard_map/ppermute | solution.py:20
  64.6 3.4 %collective-permute-start.11 = (bf16[18,18,1,256]{3,1,2,0:T(8,128)(2,1)S(1)}, bf16[18,18,1,256]{3,1,2,0:T(8,128)(2,1)S(1)}, u32[]{:S(2)}, u32[]{:S(2)}) collective-permute-start(bf16[18,18,1,256]{3,1,2,0:T(8,128)(2,1)S(1)} %copy.46), channel_id=1, source_target_pairs={{0,1},{2,3},{4,5},{6,7},{8,9},{10,11},{12,13},{14,15},{16,17},{18,... | collective-permute-start | bytes 497672 | tf_op jit(solution)/shard_map/ppermute | solution.py:17
  81.9 1.3 copy-start
Sparse Core Ops, SparseCore 0:
  110.1 92.1 all-reduce.1
where the time goes:
time: 222 us; the launch traced here: 221 us
  waiting for transfers between devices  69.7 us (31%)
  starting transfers between devices  33.6 us (15%)
  other arithmetic  31.8 us (14%)
  blocking collectives  31.3 us (14%)
  local copies, waits for them, and re-layouts  29.1 us (13%)
  between operations  14.7 us (7%)
  matrix products  11.2 us (5%)
    psum x1, waiting for transfers between devices, per_device(): gram_full, coupling = lax.psum((gram_part, couple_part), ('gx', 'gy', 'gz'))  60.8 us
    psum x1, blocking collectives, per_device(): gram_full, coupling = lax.psum((gram_part, couple_part), ('gx', 'gy', 'gz'))  31.3 us
    convert_element_type x2, other arithmetic, advance(): (centre + diffusion * laplace - 0.5 * transport).astype(jnp.bfloat16)  23.6 us
    ppermute x6, starting transfers between devices, padded_2(): lax.ppermute(lax.slice_in_dim(block, block.shape[dim] - width, None, axis...  18.9 us
    ppermute x6, starting transfers between devices, padded_2(): lax.ppermute(lax.slice_in_dim(block, 0, width, axis=dim), axis, backward)  14.7 us
    gather x1, local copies, waits for them, and re-layouts, per_device(): mean_at = jnp.take(mean_flat, obs_spots, axis=0)  11.8 us
    gather x1, local copies, waits for them, and re-layouts, per_device(): picked = jnp.take(flat_anom, obs_spots, axis=0)  9.06 us
    dot_general x16, matrix products, product(): return jnp.dot(left, right, precision=lax.Precision.HIGHEST)  7.69 us
  transfers between devices with their start and end apart: 13, of which 9 were waited for; matrix products, arithmetic and copies ran while one was open for 3% of the time, Pallas kernels for 0%

commit v1 on v0

--- a/solution.py
+++ b/solution.py
@@ -88,7 +88,10 @@
         scaled, scaled, (((0,), (0,)), ((), ())), preferred_element_type=jnp.float32
     )
     couple_part = jnp.dot(innovation, scaled, preferred_element_type=jnp.float32)
-    gram_full, coupling = lax.psum((gram_part, couple_part), ("gx", "gy", "gz"))
+    launch_group = lambda axis_key, which_axis, buf: jax.lax.psum(
+        jax.lax.psum(buf, which_axis), axis_key
+    )
+    gram_full, coupling = launch_group("gx", ("gy", "gz"), (gram_part, couple_part))
     transform = inverse_root(gram_full)
     shift = product(transform, product(transform, coupling))
     weights = (transform + shift[:, None]).astype(jnp.bfloat16)

time: 222 us -> 203 us (0.914)
  blocking collectives: 31.3 us -> 17.1 us
  waiting for transfers between devices: 69.7 us -> 62.7 us
    psum x1 -> x2, blocking collectives: 31.3 us -> 17.1 us  [the longest x1 9.92 us: per_device(): jax.lax.psum(jax.lax.psum(buf, which_axis), axis_key)]
    psum x1 -> x2, waiting for transfers between devices: 60.8 us -> 53.8 us  [the longest x1 33.2 us: per_device(): jax.lax.psum(buf, which_axis)]
  transfers between devices with their start and end apart: 13 -> 14, of which waited for: 9 -> 10; matrix products, arithmetic and copies ran while one was open for 3% -> 3% of each run, Pallas kernels for 0% -> 0%
where the time goes in v1:
time: 203 us; the launch traced here: 200 us
  waiting for transfers between devices  62.7 us (31%)
  starting transfers between devices  33.6 us (17%)
  other arithmetic  31.8 us (16%)
  local copies, waits for them, and re-layouts  29.1 us (14%)
  blocking collectives  17.1 us (8%)
  between operations  14.7 us (7%)
  matrix products  11.2 us (6%)
    psum x1, waiting for transfers between devices, per_device(): jax.lax.psum(buf, which_axis)  33.2 us
    convert_element_type x2, other arithmetic, advance(): (centre + diffusion * laplace - 0.5 * transport).astype(jnp.bfloat16)  23.6 us
    psum x1, waiting for transfers between devices, per_device(): jax.lax.psum(jax.lax.psum(buf, which_axis), axis_key)  20.6 us
    ppermute x6, starting transfers between devices, padded_2(): lax.ppermute(lax.slice_in_dim(block, block.shape[dim] - width, None, axis...  18.9 us
    ppermute x6, starting transfers between devices, padded_2(): lax.ppermute(lax.slice_in_dim(block, 0, width, axis=dim), axis, backward)  14.7 us
    gather x1, local copies, waits for them, and re-layouts, per_device(): mean_at = jnp.take(mean_flat, obs_spots, axis=0)  11.8 us
    psum x1, blocking collectives, per_device(): jax.lax.psum(jax.lax.psum(buf, which_axis), axis_key)  9.92 us
    gather x1, local copies, waits for them, and re-layouts, per_device(): picked = jnp.take(flat_anom, obs_spots, axis=0)  9.06 us
  transfers between devices with their start and end apart: 14, of which 10 were waited for; matrix products, arithmetic and copies ran while one was open for 3% of the time, Pallas kernels for 0%

profile of v1, /device:TPU:1, one launch (start us, length us, event | category | flops | bytes accessed | tf_op | source)
XLA Modules:
  0.0 200.2 jit_solution(3066018443840979386)
XLA Ops:
  6.5 1.0 fusion.37
  7.5 4.0 %collective-permute-start.1 = (bf16[1,16,16,256]{3,2,1,0:T(8,128)(2,1)S(1)}, bf16[1,16,16,256]{3,2,1,0:T(8,128)(2,1)S(1)}, u32[]{:S(2)}, u32[]{:S(2)}) collective-permute-start(bf16[1,16,16,256]{3,2,1,0:T(8,128)(2,1)S(1)} %get-tuple-element.18), channel_id=1, source_target_pairs={{0,4},{4,8},{8,12},{1,5},{5,9},{9,13},{2,6},{6,10},{10,14},{3,7},{... | collective-permute-start | bytes 393224 | tf_op jit(solution)/shard_map/ppermute | solution.py:17
  11.6 1.3 collective-permute-start
  12.9 0.8 collective-permute-done.1
  13.7 1.8 constant_dynamic-update-slice_fusion.1
  15.6 1.7 collective-permute-done
  17.3 1.3 collective-permute-start.2
  18.6 4.0 %collective-permute-start.3 = (bf16[18,1,16,256]{3,2,1,0:T(8,128)(2,1)S(1)}, bf16[18,1,16,256]{3,2,1,0:T(8,128)(2,1)S(1)}, u32[]{:S(2)}, u32[]{:S(2)}) collective-permute-start(bf16[18,1,16,256]{3,2,1,0:T(8,128)(2,1)S(1)} %get-tuple-element.13), channel_id=1, source_target_pairs={{0,2},{1,3},{4,6},{5,7},{8,10},{9,11},{12,14},{13,15},{16,18},{17,... | collective-permute-start | bytes 442376 | tf_op jit(solution)/shard_map/ppermute | solution.py:17
  22.7 0.1 reshape.81
  22.9 0.3 collective-permute-done.2
  23.2 1.5 collective-permute-done.3
  24.7 0.5 pad_maximum_fusion.35
  25.3 5.2 %collective-permute-start.4 = (bf16[18,18,1,256]{3,1,2,0:T(8,128)(2,1)S(1)}, bf16[18,18,1,256]{3,1,2,0:T(8,128)(2,1)S(1)}, u32[]{:S(2)}, u32[]{:S(2)}) collective-permute-start(bf16[18,18,1,256]{3,1,2,0:T(8,128)(2,1)S(1)} %copy.40), channel_id=1, source_target_pairs={{1,0},{3,2},{5,4},{7,6},{9,8},{11,10},{13,12},{15,14},{17,16},{19,... | collective-permute-start | bytes 497672 | tf_op jit(solution)/shard_map/ppermute | solution.py:20
  30.5 1.4 collective-permute-start.5
  32.0 1.1 slice_bitcast_fusion.2
  33.0 0.3 copy.41
  33.3 0.7 collective-permute-done.5
  34.0 0.3 copy.43
  34.3 10.0 %fusion.6 = bf16[16,16,16,256]{3,2,1,0:T(8,128)(2,1)S(1)} fusion(bf16[16,16,16,256]{3,2,1,0:T(8,128)(2,1)S(1)} %copy-done.3, bf16[18,18,1,256]{3,2,1,0:T(2,128)(2,1)S(1)} %copy.43, bf16[18,1,16,256]{3,2,1,0:T(8,128)(2,1)S(1)} %collective-permute-done.2, bf16[18,16,16,256]{3,2,1,0:T(8,128)(2,1)S(1)} %copy-done.2, ...), kind=kLoop, calls=%fused_computation.33 | loop fusion | flops 57671680 | bytes 7491584 | tf_op jit(solution)/shard_map/convert_element_type | solution.py:38
  44.3 1.3 collective-permute-start.6
  45.6 4.0 %collective-permute-start.7 = (bf16[1,16,16,256]{3,2,1,0:T(8,128)(2,1)S(1)}, bf16[1,16,16,256]{3,2,1,0:T(8,128)(2,1)S(1)}, u32[]{:S(2)}, u32[]{:S(2)}) collective-permute-start(bf16[1,16,16,256]{3,2,1,0:T(8,128)(2,1)S(1)} %get-tuple-element.15), channel_id=1, source_target_pairs={{0,4},{4,8},{8,12},{1,5},{5,9},{9,13},{2,6},{6,10},{10,14},{3,7},{... | collective-permute-start | bytes 393224 | tf_op jit(solution)/shard_map/ppermute | solution.py:17
  49.7 1.1 collective-permute-done.6
  50.9 0.9 collective-permute-done.7
  51.8 1.3 collective-permute-start.8
  53.1 4.1 %collective-permute-start.9 = (bf16[18,1,16,256]{3,2,1,0:T(8,128)(2,1)S(1)}, bf16[18,1,16,256]{3,2,1,0:T(8,128)(2,1)S(1)}, u32[]{:S(2)}, u32[]{:S(2)}) collective-permute-start(bf16[18,1,16,256]{3,2,1,0:T(8,128)(2,1)S(1)} %get-tuple-element.11), channel_id=1, source_target_pairs={{0,2},{1,3},{4,6},{5,7},{8,10},{9,11},{12,14},{13,15},{16,18},{17,... | collective-permute-start | bytes 442376 | tf_op jit(solution)/shard_map/ppermute | solution.py:17
  57.2 0.9 convert_multiply_fusion.4
  58.3 0.9 copy.54
  59.3 0.7 pad_maximum_fusion.32
  60.1 4.4 %collective-permute-start.10 = (bf16[18,18,1,256]{3,1,2,0:T(8,128)(2,1)S(1)}, bf16[18,18,1,256]{3,1,2,0:T(8,128)(2,1)S(1)}, u32[]{:S(2)}, u32[]{:S(2)}) collective-permute-start(bf16[18,18,1,256]{3,1,2,0:T(8,128)(2,1)S(1)} %copy.44), channel_id=1, source_target_pairs={{1,0},{3,2},{5,4},{7,6},{9,8},{11,10},{13,12},{15,14},{17,16},{19,... | collective-permute-start | bytes 497672 | tf_op jit(solution)/shard_map/ppermute | solution.py:20
  64.6 1.3 collective-permute-start.11
  65.9 0.3 copy.45
  66.2 1.8 collective-permute-done.11
  67.9 0.3 copy.47
  68.2 13.7 %fusion.16 = bf16[16,16,16,256]{3,2,1,0:T(8,128)(2,1)S(1)} fusion(bf16[16,16,16,256]{3,2,1,0:T(8,128)(2,1)S(1)} %fusion.6, bf16[18,18,1,256]{3,2,1,0:T(2,128)(2,1)S(1)} %copy.47, bf16[18,1,16,256]{3,2,1,0:T(8,128)(2,1)S(1)} %collective-permute-done.8, bf16[18,1,16,256]{3,2,1,0:T(8,128)(2,1)S(1)} %collective-permute-done.9, ...), kind=kLoop, calls=%fused_computation.43 | loop fusion | flops 74448896 | bytes 5132288 | tf_op jit(solution)/shard_map/convert_element_type | solution.py:38
  81.9 1.3 copy-done
  83.2 0.6 convert_reduce_fusion
  84.0 1.9 fusion.21
  86.1 9.1 %gather_fusion = bf16[2048,256]{1,0:T(8,128)(2,1)} fusion(bf16[4096,256]{1,0:T(8,128)(2,1)S(1)} %bitcast.48, s32[2048]{0:T(1024)S(1)} %broadcast_clamp_fusion), kind=kCustom, calls=%fused_computation | custom fusion | bytes 2105344 | tf_op jit(solution)/shard_map/jit(_take)/gather | solution.py:75
  95.2 11.8 %gather_fusion.1 = f32[2048]{0:T(1024)S(1)} fusion(f32[4096]{0:T(1024)S(1)} %div.28, s32[2048]{0:T(1024)S(1)} %broadcast_clamp_fusion), kind=kCustom, calls=%fused_computation.1 | custom fusion | bytes 24576 | tf_op jit(solution)/shard_map/jit(_take)/gather | solution.py:76
  107.0 1.8 multiply_convert_fusion
  108.7 1.2 fusion.38
  110.0 33.2 %all-reduce.3.cloned.1.call-done = f32[256,256]{1,0:T(8,128)} async-done(((f32[256,256]{1,0:T(8,128)}), f32[256,256]{1,0:T(8,128)}) %all-reduce.3.cloned.1.call-update) | async-done | bytes 262160 | tf_op jit(solution)/shard_map/psum | solution.py:92
  143.2 0.2 fusion.45
  143.4 7.2 %psum.30 = f32[256]{0:T(256)S(1)} all-reduce(f32[256]{0:T(256)S(1)} %bitcast.53), channel_id=1, replica_groups=mesh['grp'=2,'gx'=4,'gy'=2,'gz'=2] {'gy','gz'}, use_global_device_ids=true, to_apply=%region_4.5 | all-reduce | flops 256 | bytes 2048 | tf_op jit(solution)/shard_map/psum | solution.py:92
  150.6 9.9 %psum.31 = f32[256]{0:T(256)S(1)} all-reduce(f32[256]{0:T(256)S(1)} %psum.30), channel_id=1, replica_groups=mesh['grp'=2,'gx'=4,'gy'=2,'gz'=2] {'gx'}, use_global_device_ids=true, to_apply=%region_5.6 | all-reduce | flops 256 | bytes 2048 | tf_op jit(solution)/shard_map/psum | solution.py:91
  160.5 20.6 %all-reduce.5.cloned.1.call-done = f32[256,256]{1,0:T(8,128)} async-done(((f32[256,256]{1,0:T(8,128)}), f32[256,256]{1,0:T(8,128)}) %all-reduce.5.cloned.1.call-update) | async-done | bytes 262160 | tf_op jit(solution)/shard_map/psum | solution.py:91
  181.1 1.6 multiply_reduce_fusion
  183.4 1.3 fusion.28
  184.7 0.3 fusion.29
  185.0 1.4 fusion.32
  186.4 0.4 fusion.27
  186.8 0.4 fusion.40
  187.2 0.4 fusion.39
  187.5 0.4 fusion.26
  187.9 0.4 fusion.42
  188.3 0.4 fusion.41
  188.7 0.4 fusion.25
  189.1 0.4 fusion.44
  189.5 0.4 fusion.43
  189.9 0.4 fusion.24
  190.3 0.4 convolution_divide_fusion
  190.7 0.3 convolution_bitcast_fusion
  191.0 0.3 fusion.46
  191.3 2.1 %fusion = bf16[4096,256]{1,0:T(8,128)(2,1)} fusion(bf16[4096,256]{1,0:T(8,128)(2,1)S(1)} %bitcast.49, f32[4096]{0:T(1024)S(1)} %div.28, f32[256,256]{1,0:T(8,128)S(1)} %convolution_divide_fusion, f32[256]{0:T(256)S(1)} %bitcast.51), kind=kOutput, calls=%fused_computation.27 | convolution fusion | flops 539099136 | bytes 4473856 | tf_op jit(solution)/shard_map/dot_general | solution.py:98
  (39 shorter events, 1.2 us)
Async XLA Ops:
  6.5 136.6 %all-reduce.3.cloned.1.call-start = ((), (), s32[]{:S(2)}) async-start(), calls=%async_computation | async-start | bytes 524288 | tf_op jit(solution)/shard_map/psum | solution.py:92
  7.5 6.2 %collective-permute-start.1 = (bf16[1,16,16,256]{3,2,1,0:T(8,128)(2,1)S(1)}, bf16[1,16,16,256]{3,2,1,0:T(8,128)(2,1)S(1)}, u32[]{:S(2)}, u32[]{:S(2)}) collective-permute-start(bf16[1,16,16,256]{3,2,1,0:T(8,128)(2,1)S(1)} %get-tuple-element.18), channel_id=1, source_target_pairs={{0,4},{4,8},{8,12},{1,5},{5,9},{9,13},{2,6},{6,10},{10,14},{3,7},{... | collective-permute-start | bytes 393224 | tf_op jit(solution)/shard_map/ppermute | solution.py:17
  11.6 5.7 %collective-permute-start = (bf16[1,16,16,256]{3,2,1,0:T(8,128)(2,1)S(1)}, bf16[1,16,16,256]{3,2,1,0:T(8,128)(2,1)S(1)}, u32[]{:S(2)}, u32[]{:S(2)}) collective-permute-start(bf16[1,16,16,256]{3,2,1,0:T(8,128)(2,1)S(1)} %get-tuple-element.17), channel_id=1, source_target_pairs={{4,0},{8,4},{12,8},{5,1},{9,5},{13,9},{6,2},{10,6},{14,10},{7,3},{... | collective-permute-start | bytes 393224 | tf_op jit(solution)/shard_map/ppermute | solution.py:20
  13.7 8.9 %copy-start.4 = (s32[16,16,8]{1,2,0:T(8,128)S(1)}, s32[16,16,8]{1,2,0:T(8,128)}, u32[]{:S(2)}) copy-start(s32[16,16,8]{1,2,0:T(8,128)} %param.10) | copy-start | bytes 24580
  17.3 8.0 %copy-start.1 = (bf16[18,16,16,256]{3,2,1,0:T(8,128)(2,1)}, bf16[18,16,16,256]{3,2,1,0:T(8,128)(2,1)S(1)}, u32[]{:S(2)}) copy-start(bf16[18,16,16,256]{3,2,1,0:T(8,128)(2,1)S(1)} %constant_dynamic-update-slice_fusion) | copy-start | bytes 7077892
  17.3 5.9 %collective-permute-start.2 = (bf16[18,1,16,256]{3,2,1,0:T(8,128)(2,1)S(1)}, bf16[18,1,16,256]{3,2,1,0:T(8,128)(2,1)S(1)}, u32[]{:S(2)}, u32[]{:S(2)}) collective-permute-start(bf16[18,1,16,256]{3,2,1,0:T(8,128)(2,1)S(1)} %get-tuple-element.14), channel_id=1, source_target_pairs={{2,0},{3,1},{6,4},{7,5},{10,8},{11,9},{14,12},{15,13},{18,16},{19,... | collective-permute-start | bytes 442376 | tf_op jit(solution)/shard_map/ppermute | solution.py:20
  18.6 6.1 %collective-permute-start.3 = (bf16[18,1,16,256]{3,2,1,0:T(8,128)(2,1)S(1)}, bf16[18,1,16,256]{3,2,1,0:T(8,128)(2,1)S(1)}, u32[]{:S(2)}, u32[]{:S(2)}) collective-permute-start(bf16[18,1,16,256]{3,2,1,0:T(8,128)(2,1)S(1)} %get-tuple-element.13), channel_id=1, source_target_pairs={{0,2},{1,3},{4,6},{5,7},{8,10},{9,11},{12,14},{13,15},{16,18},{17,... | collective-permute-start | bytes 442376 | tf_op jit(solution)/shard_map/ppermute | solution.py:17
  22.9 11.4 %copy-start.3 = (bf16[16,16,16,256]{3,2,1,0:T(8,128)(2,1)S(1)}, bf16[16,16,16,256]{3,2,1,0:T(8,128)(2,1)}, u32[]{:S(2)}) copy-start(bf16[16,16,16,256]{3,2,1,0:T(8,128)(2,1)} %param.6) | copy-start | bytes 6291460
  25.3 7.7 %collective-permute-start.4 = (bf16[18,18,1,256]{3,1,2,0:T(8,128)(2,1)S(1)}, bf16[18,18,1,256]{3,1,2,0:T(8,128)(2,1)S(1)}, u32[]{:S(2)}, u32[]{:S(2)}) collective-permute-start(bf16[18,18,1,256]{3,1,2,0:T(8,128)(2,1)S(1)} %copy.40), channel_id=1, source_target_pairs={{1,0},{3,2},{5,4},{7,6},{9,8},{11,10},{13,12},{15,14},{17,16},{19,... | collective-permute-start | bytes 497672 | tf_op jit(solution)/shard_map/ppermute | solution.py:20
  30.5 3.8 %copy-start.2 = (bf16[18,16,16,256]{3,2,1,0:T(8,128)(2,1)S(1)}, bf16[18,16,16,256]{3,2,1,0:T(8,128)(2,1)}, u32[]{:S(2)}) copy-start(bf16[18,16,16,256]{3,2,1,0:T(8,128)(2,1)} %copy-done.1) | copy-start | bytes 7077892
  30.5 3.5 %collective-permute-start.5 = (bf16[18,18,1,256]{3,1,2,0:T(8,128)(2,1)S(1)}, bf16[18,18,1,256]{3,1,2,0:T(8,128)(2,1)S(1)}, u32[]{:S(2)}, u32[]{:S(2)}) collective-permute-start(bf16[18,18,1,256]{3,1,2,0:T(8,128)(2,1)S(1)} %copy.42), channel_id=1, source_target_pairs={{0,1},{2,3},{4,5},{6,7},{8,9},{10,11},{12,13},{14,15},{16,17},{18,... | collective-permute-start | bytes 497672 | tf_op jit(solution)/shard_map/ppermute | solution.py:17
  44.3 6.5 %collective-permute-start.6 = (bf16[1,16,16,256]{3,2,1,0:T(8,128)(2,1)S(1)}, bf16[1,16,16,256]{3,2,1,0:T(8,128)(2,1)S(1)}, u32[]{:S(2)}, u32[]{:S(2)}) collective-permute-start(bf16[1,16,16,256]{3,2,1,0:T(8,128)(2,1)S(1)} %get-tuple-element.16), channel_id=1, source_target_pairs={{4,0},{8,4},{12,8},{5,1},{9,5},{13,9},{6,2},{10,6},{14,10},{7,3},{... | collective-permute-start | bytes 393224 | tf_op jit(solution)/shard_map/ppermute | solution.py:20
  45.6 6.1 %collective-permute-start.7 = (bf16[1,16,16,256]{3,2,1,0:T(8,128)(2,1)S(1)}, bf16[1,16,16,256]{3,2,1,0:T(8,128)(2,1)S(1)}, u32[]{:S(2)}, u32[]{:S(2)}) collective-permute-start(bf16[1,16,16,256]{3,2,1,0:T(8,128)(2,1)S(1)} %get-tuple-element.15), channel_id=1, source_target_pairs={{0,4},{4,8},{8,12},{1,5},{5,9},{9,13},{2,6},{6,10},{10,14},{3,7},{... | collective-permute-start | bytes 393224 | tf_op jit(solution)/shard_map/ppermute | solution.py:17
  51.8 7.6 %collective-permute-start.8 = (bf16[18,1,16,256]{3,2,1,0:T(8,128)(2,1)S(1)}, bf16[18,1,16,256]{3,2,1,0:T(8,128)(2,1)S(1)}, u32[]{:S(2)}, u32[]{:S(2)}) collective-permute-start(bf16[18,1,16,256]{3,2,1,0:T(8,128)(2,1)S(1)} %get-tuple-element.12), channel_id=1, source_target_pairs={{2,0},{3,1},{6,4},{7,5},{10,8},{11,9},{14,12},{15,13},{18,16},{19,... | collective-permute-start | bytes 442376 | tf_op jit(solution)/shard_map/ppermute | solution.py:20
  53.1 6.3 %collective-permute-start.9 = (bf16[18,1,16,256]{3,2,1,0:T(8,128)(2,1)S(1)}, bf16[18,1,16,256]{3,2,1,0:T(8,128)(2,1)S(1)}, u32[]{:S(2)}, u32[]{:S(2)}) collective-permute-start(bf16[18,1,16,256]{3,2,1,0:T(8,128)(2,1)S(1)} %get-tuple-element.11), channel_id=1, source_target_pairs={{0,2},{1,3},{4,6},{5,7},{8,10},{9,11},{12,14},{13,15},{16,18},{17,... | collective-permute-start | bytes 442376 | tf_op jit(solution)/shard_map/ppermute | solution.py:17
  60.1 5.8 %collective-permute-start.10 = (bf16[18,18,1,256]{3,1,2,0:T(8,128)(2,1)S(1)}, bf16[18,18,1,256]{3,1,2,0:T(8,128)(2,1)S(1)}, u32[]{:S(2)}, u32[]{:S(2)}) collective-permute-start(bf16[18,18,1,256]{3,1,2,0:T(8,128)(2,1)S(1)} %copy.44), channel_id=1, source_target_pairs={{1,0},{3,2},{5,4},{7,6},{9,8},{11,10},{13,12},{15,14},{17,16},{19,... | collective-permute-start | bytes 497672 | tf_op jit(solution)/shard_map/ppermute | solution.py:20
  64.6 3.4 %collective-permute-start.11 = (bf16[18,18,1,256]{3,1,2,0:T(8,128)(2,1)S(1)}, bf16[18,18,1,256]{3,1,2,0:T(8,128)(2,1)S(1)}, u32[]{:S(2)}, u32[]{:S(2)}) collective-permute-start(bf16[18,18,1,256]{3,1,2,0:T(8,128)(2,1)S(1)} %copy.46), channel_id=1, source_target_pairs={{0,1},{2,3},{4,5},{6,7},{8,9},{10,11},{12,13},{14,15},{16,17},{18,... | collective-permute-start | bytes 497672 | tf_op jit(solution)/shard_map/ppermute | solution.py:17
  81.9 1.3 copy-start
  109.9 71.2 %all-reduce.5.cloned.1.call-start = ((), (), s32[]{:S(2)}) async-start(), calls=%async_computation.1 | async-start | bytes 524288 | tf_op jit(solution)/shard_map/psum | solution.py:91
Sparse Core Ops, SparseCore 0:
  110.0 33.0 all-reduce.2
  145.6 35.4 all-reduce.4
